TPU v7x, 32 devices: a whole 2x2x4 slice. The times are simulated.
32 devices in a mesh: group: 2 (over y), section: 4 (over z), dp: 4 (over x, core).
Axes of the slice: x: 2, y: 2, z: 4, core: 2. Of those that a mesh axis runs over, the one named last changes fastest.
Arguments:
- tokens: bfloat16 [4, 8, 32, 1600], P(None, ('group', 'dp')), parts along dimension 1, may hold values from -6 to 6
- pixel_index: int32 [4, 8, 384], P(None, ('group', 'dp')), parts along dimension 1, may hold values from 0 to 6271
- point_mask: int32 [4, 8, 384], P(None, ('group', 'dp')), parts along dimension 1, may hold values from 0 to 1, as said below
- point_depth: float32 [4, 8, 384], P(None, ('group', 'dp')), parts along dimension 1, may hold values from -6 to 6
- hook_section: int32 [4], replicated, may hold values from 0 to 2, as said below
- w_query: bfloat16 [4, 1600, 832], P('section')
- w_key: bfloat16 [4, 1600, 832], P('section')
- w_value: bfloat16 [4, 1600, 832], P('section'), may hold values from -0.15625 to 0.15625
- w_output: bfloat16 [4, 832, 1600], P('section'), may hold values from -0.21875 to 0.21875
- reassemble: bfloat16 [5, 1600, 128], P(None, None, ('section', 'dp')), may hold values from -0.15625 to 0.15625
- merging: bfloat16 [4, 128, 128], P(None, None, ('section', 'dp')), may hold values from -0.5 to 0.5
- predict: bfloat16 [128, 196], P(('section', 'dp')), may hold values from -0.5 to 0.5
Outputs:
- grad_query: bfloat16 [8, 1600, 832], P(('group', 'section'), 'dp'), parts along dimension 0
- grad_key: bfloat16 [8, 1600, 832], P(('group', 'section'), 'dp'), parts along dimension 0
- grad_value: bfloat16 [8, 1600, 832], P(('group', 'section'), 'dp'), parts along dimension 0
- grad_output: bfloat16 [8, 832, 1600], P(('group', 'section'), 'dp'), parts along dimension 0
- grad_reassemble: float32 [10, 1600, 128], P('group', None, ('section', 'dp')), parts along dimension 0
- grad_merging: float32 [8, 128, 128], P('group', None, ('section', 'dp')), parts along dimension 0
- grad_predict: float32 [256, 196], P(('group', 'section', 'dp')), parts along dimension 0
There are 2 independent parts, one for each index of `group`. A program takes and returns all parts, laid end to end along the dimension named above; an argument that names none is the same for every part. Nothing has to cross between parts.
Inputs may be any that keep to these rules, and one draw needn't show every extreme that they name: `point_mask`: in each image the valid points come first, and at least 48 of them are valid. `hook_section`: Sorted; the last entry is 2.
All inputs are finite; a program needn't handle non-finite values.
Results may differ from a plain program's by a relative error of at most 0.03.
Values may be sent and summed in bfloat16 or wider, within the bound.
A program may use at most 128 MiB of HBM per device.

v0:
```python
import math

import jax
import jax.numpy as jnp
from jax import lax
from jax.sharding import PartitionSpec as P

HEADS = 13
NHOOK = 4


EPS = 1e-06


def passed_along(block, axis, distance):
    devices = range(lax.axis_size(axis))
    route = [(i - distance, i) for i in devices if i - distance in devices]
    return lax.ppermute(block, axis, route)


def broadcast(value, axis, source):
    kept = jnp.where(lax.axis_index(axis) == source, value, 0).astype(value.dtype)
    return lax.psum(kept, axis)


def as_sent(x):
    return jax.tree.map(lambda a: a.astype(jnp.bfloat16) if a.dtype == jnp.float32 else a, x)


def rms_normed(stream):
    widened = stream.astype(jnp.float32)
    inv_root = lax.rsqrt(jnp.mean(widened * widened, axis=-1, keepdims=True) + EPS)
    return (widened * inv_root).astype(jnp.bfloat16)


def attend(query_rows, key_rows, value_rows):
    image_count, token_count, inner_width = query_rows.shape
    head_width = inner_width // HEADS
    shape_heads = (image_count, token_count, HEADS, head_width)
    query_heads = query_rows.astype(jnp.float32).reshape(shape_heads)
    key_heads = key_rows.astype(jnp.float32).reshape(shape_heads)
    value_heads = value_rows.astype(jnp.float32).reshape(shape_heads)
    scores = jnp.einsum("bqhe,bkhe->bhqk", query_heads, key_heads) / math.sqrt(head_width)
    probabilities = jax.nn.softmax(scores, axis=-1).astype(jnp.bfloat16)
    mixed_heads = jnp.einsum("bhqk,bkhe->bqhe", probabilities.astype(jnp.float32), value_heads)
    return mixed_heads.reshape(image_count, token_count, inner_width).astype(jnp.bfloat16)


def attention_layer(stream, layer_query, layer_key, layer_value, layer_output, nudges):
    image_count, token_count, model_width = stream.shape
    normed = rms_normed(stream).reshape(image_count * token_count, model_width)
    query_rows = (
        jnp.dot(normed, layer_query, preferred_element_type=jnp.float32).astype(jnp.bfloat16)
        + nudges[0]
    )
    key_rows = (
        jnp.dot(normed, layer_key, preferred_element_type=jnp.float32).astype(jnp.bfloat16)
        + nudges[1]
    )
    value_rows = (
        jnp.dot(normed, layer_value, preferred_element_type=jnp.float32).astype(jnp.bfloat16)
        + nudges[2]
    )
    inner_width = layer_query.shape[1]
    mixed = attend(
        query_rows.reshape(image_count, token_count, inner_width),
        key_rows.reshape(image_count, token_count, inner_width),
        value_rows.reshape(image_count, token_count, inner_width),
    )
    mixed_rows = mixed.reshape(image_count * token_count, inner_width)
    update = jnp.dot(mixed_rows, layer_output, preferred_element_type=jnp.float32)
    update = update.reshape(image_count, token_count, model_width)
    output_rows = stream.astype(jnp.float32) + update
    return (output_rows, (normed, mixed_rows))


def reassemble_map(features, weight):
    flat_rows = features.reshape(-1, features.shape[-1]).astype(jnp.bfloat16)
    return jnp.dot(flat_rows, weight, preferred_element_type=jnp.float32).astype(jnp.bfloat16)


def head_rest(projected, top_projected, merging, predict, pixel_index, point_mask, point_depth):
    merged = top_projected.astype(jnp.float32)
    for hook_slot in range(len(projected) - 1, -1, -1):
        activated = jax.nn.silu(merged).astype(jnp.bfloat16)
        merged = projected[hook_slot].astype(jnp.float32) + jnp.dot(
            activated, merging[hook_slot], preferred_element_type=jnp.float32
        )
    activated = jax.nn.silu(merged).astype(jnp.bfloat16)
    depth_rows = jnp.dot(activated, predict, preferred_element_type=jnp.float32)
    depth_map = depth_rows.reshape(pixel_index.shape[0], pixel_index.shape[1], -1)
    picked = jnp.take_along_axis(depth_map, pixel_index, axis=2)
    valid_mask = point_mask.astype(jnp.float32)
    valid_count = jnp.sum(valid_mask, axis=2)
    misfit = (picked - point_depth) * valid_mask
    return jnp.sum(jnp.sum(misfit * misfit, axis=2) / valid_count)


def keep_rows(stream):
    return stream


def put_slot(store_array, item_rows, micro_slot, active):
    updated = lax.dynamic_update_index_in_dim(store_array, item_rows, micro_slot, 0)
    return jnp.where(active, updated, store_array)


def contract(left_rows, right_rows):
    return jnp.einsum("mrd,mrh->dh", left_rows, right_rows, preferred_element_type=jnp.float32)


def on_device(
    tokens,
    pixel_index,
    point_mask,
    point_depth,
    hook_section,
    w_query,
    w_key,
    w_value,
    w_output,
    reassemble,
    merging,
    predict,
):
    section_index = lax.axis_index("section")
    section_count = lax.axis_size("section")
    last_section = section_count - 1
    is_last = section_index == last_section
    micro_count = tokens.shape[0]
    token_rows = tokens.shape[1] * tokens.shape[2]
    model_width = tokens.shape[3]
    inner_width = w_query.shape[2]
    layer_query = w_query[0]
    layer_key = w_key[0]
    layer_value = w_value[0]
    layer_output = w_output[0]
    full_reassemble, full_merging, full_predict = (
        lax.all_gather(reassemble, ("section", "dp"), axis=2, tiled=True),
        lax.all_gather(merging, ("section", "dp"), axis=2, tiled=True),
        lax.all_gather(predict, ("section", "dp"), axis=0, tiled=True),
    )
    zero_nudges = jnp.zeros((3, token_rows, inner_width), jnp.bfloat16)
    zero_rows = jnp.zeros(tokens.shape[1:], jnp.float32)
    empty_store = jnp.zeros(tokens.shape, jnp.float32)

    def run_layer(stream):
        return attention_layer(
            stream, layer_query, layer_key, layer_value, layer_output, zero_nudges
        )[0]

    def forward_step(time_step, carried):
        incoming, inputs_store, outputs_store = carried
        micro_index = time_step - section_index
        active = jnp.logical_and(micro_index >= 0, micro_index < micro_count)
        micro_slot = jnp.clip(micro_index, 0, micro_count - 1)
        fresh_rows = lax.dynamic_index_in_dim(tokens, micro_slot, 0, keepdims=False).astype(
            jnp.float32
        )
        source = jnp.where(section_index == 0, fresh_rows, incoming)
        result = lax.cond(active, run_layer, keep_rows, source)
        inputs_store = put_slot(inputs_store, source, micro_slot, active)
        outputs_store = put_slot(outputs_store, result, micro_slot, active)
        incoming = passed_along(result, "section", 1)
        return (incoming, inputs_store, outputs_store)

    unused, inputs_store, outputs_store = lax.fori_loop(
        0, micro_count + section_count - 1, forward_step, (zero_rows, empty_store, empty_store)
    )
    hook_sum = jnp.zeros(tokens.shape, jnp.float32)
    received = []
    for hook_slot in range(NHOOK):
        local_piece = reassemble_map(outputs_store, full_reassemble[hook_slot])
        received.append(broadcast(local_piece, "section", hook_section[hook_slot]))
    projected_in = tuple(received)

    def head_grads(head_items):

        def loss_terms(projected, top_feature, reassemble_last, head_merging, head_predict):
            top_projected = reassemble_map(top_feature, reassemble_last)
            return head_rest(
                projected,
                top_projected,
                head_merging,
                head_predict,
                pixel_index,
                point_mask,
                point_depth,
            )

        loss_value, pullback = jax.vjp(
            loss_terms,
            head_items[0],
            head_items[1],
            full_reassemble[NHOOK],
            full_merging,
            full_predict,
        )
        return pullback(jnp.ones((), jnp.float32))

    def no_grads(head_items):
        return (
            tuple((jnp.zeros_like(array_item) for array_item in head_items[0])),
            jnp.zeros_like(head_items[1]),
            jnp.zeros_like(full_reassemble[NHOOK]),
            jnp.zeros_like(full_merging),
            jnp.zeros_like(full_predict),
        )

    projected_grads, last_grad, reassemble_last_grad, grad_merging, grad_predict = lax.cond(
        is_last, head_grads, no_grads, (projected_in, outputs_store)
    )
    projected_cotangents = broadcast(jnp.stack(projected_grads), "section", last_section)
    weight_grads = []
    for hook_slot in range(NHOOK):
        unused_rows, pullback = jax.vjp(reassemble_map, outputs_store, full_reassemble[hook_slot])
        feature_grad, weight_grad = pullback(projected_cotangents[hook_slot])
        is_owner = hook_section[hook_slot] == section_index
        hook_sum = hook_sum + jnp.where(is_owner, feature_grad, 0.0)
        weight_grads.append(jnp.where(is_owner, weight_grad, jnp.zeros_like(weight_grad)))
    weight_grads.append(reassemble_last_grad)
    grad_reassemble = jnp.stack(weight_grads)
    hook_grad = hook_sum

    def backward_one(stream, cotangent):

        def local_layer(entry_rows, nudges):
            return attention_layer(
                entry_rows, layer_query, layer_key, layer_value, layer_output, nudges
            )

        unused_rows, pullback, saved = jax.vjp(local_layer, stream, zero_nudges, has_aux=True)
        entry_grad, nudge_grad = pullback(cotangent)
        return (entry_grad, nudge_grad, saved[0], saved[1])

    def skip_one(stream, cotangent):
        return (
            jnp.zeros_like(stream),
            zero_nudges,
            jnp.zeros((token_rows, model_width), jnp.bfloat16),
            jnp.zeros((token_rows, inner_width), jnp.bfloat16),
        )

    def backward_step(time_step, carried):
        incoming, nudge_store, normed_store, mixed_store, cotangent_store = carried
        micro_index = time_step - (last_section - section_index)
        active = jnp.logical_and(micro_index >= 0, micro_index < micro_count)
        micro_slot = jnp.clip(micro_index, 0, micro_count - 1)
        upstream = jnp.where(
            is_last, lax.dynamic_index_in_dim(last_grad, micro_slot, 0, keepdims=False), incoming
        )
        cotangent = upstream + lax.dynamic_index_in_dim(hook_grad, micro_slot, 0, keepdims=False)
        stream = lax.dynamic_index_in_dim(inputs_store, micro_slot, 0, keepdims=False)
        entry_grad, nudge_grad, normed, mixed_rows = lax.cond(
            active, backward_one, skip_one, stream, cotangent
        )
        nudge_store = put_slot(nudge_store, nudge_grad, micro_slot, active)
        normed_store = put_slot(normed_store, normed, micro_slot, active)
        mixed_store = put_slot(mixed_store, mixed_rows, micro_slot, active)
        cotangent_store = put_slot(cotangent_store, cotangent, micro_slot, active)
        incoming = jax.tree.map(
            lambda part, own: part.astype(own.dtype),
            passed_along(as_sent(entry_grad), "section", -1),
            entry_grad,
        )
        return (incoming, nudge_store, normed_store, mixed_store, cotangent_store)

    start_state = (
        zero_rows,
        jnp.zeros((micro_count, 3, token_rows, inner_width), jnp.bfloat16),
        jnp.zeros((micro_count, token_rows, model_width), jnp.bfloat16),
        jnp.zeros((micro_count, token_rows, inner_width), jnp.bfloat16),
        empty_store,
    )
    unused, nudge_store, normed_store, mixed_store, cotangent_store = lax.fori_loop(
        0, micro_count + section_count - 1, backward_step, start_state
    )
    grad_query = contract(normed_store, nudge_store[:, 0])
    grad_key = contract(normed_store, nudge_store[:, 1])
    grad_value = contract(normed_store, nudge_store[:, 2])
    mixed_all = mixed_store.reshape(micro_count * token_rows, inner_width)
    update_grad = cotangent_store.reshape(micro_count * token_rows, model_width)

    def output_map(weight):
        return jnp.dot(mixed_all, weight, preferred_element_type=jnp.float32)

    unused_update, output_pullback = jax.vjp(output_map, layer_output)
    grad_output = output_pullback(update_grad)[0].astype(jnp.float32)
    summed_query, summed_key, summed_value, summed_output = (
        lax.psum_scatter(
            grad_query[None].astype(jnp.bfloat16), "dp", scatter_dimension=1, tiled=True
        ).astype(jnp.float32),
        lax.psum_scatter(
            grad_key[None].astype(jnp.bfloat16), "dp", scatter_dimension=1, tiled=True
        ).astype(jnp.float32),
        lax.psum_scatter(
            grad_value[None].astype(jnp.bfloat16), "dp", scatter_dimension=1, tiled=True
        ).astype(jnp.float32),
        lax.psum_scatter(
            grad_output[None].astype(jnp.bfloat16), "dp", scatter_dimension=1, tiled=True
        ).astype(jnp.float32),
    )
    head_reassemble, head_merging, head_predict = (
        lax.psum_scatter(
            grad_reassemble.astype(jnp.float32), ("section", "dp"), scatter_dimension=2, tiled=True
        ),
        lax.psum_scatter(
            grad_merging.astype(jnp.float32), ("section", "dp"), scatter_dimension=2, tiled=True
        ),
        lax.psum_scatter(
            grad_predict.astype(jnp.float32), ("section", "dp"), scatter_dimension=0, tiled=True
        ),
    )
    return (
        summed_query.astype(jnp.bfloat16),
        summed_key.astype(jnp.bfloat16),
        summed_value.astype(jnp.bfloat16),
        summed_output.astype(jnp.bfloat16),
        head_reassemble,
        head_merging,
        head_predict,
    )


def solution(mesh):
    placed = (
        P(None, ("group", "dp"), None, None),
        P(None, ("group", "dp"), None),
        P(None, ("group", "dp"), None),
        P(None, ("group", "dp"), None),
        P(),
        P("section", None, None),
        P("section", None, None),
        P("section", None, None),
        P("section", None, None),
        P(None, None, ("section", "dp")),
        P(None, None, ("section", "dp")),
        P(("section", "dp"), None),
    )
    return jax.shard_map(
        on_device,
        mesh=mesh,
        in_specs=placed,
        out_specs=(
            P(("group", "section"), "dp", None),
            P(("group", "section"), "dp", None),
            P(("group", "section"), "dp", None),
            P(("group", "section"), "dp", None),
            P("group", None, ("section", "dp")),
            P("group", None, ("section", "dp")),
            P(("group", "section", "dp"), None),
        ),
        check_vma=False,
    )
```

profile of v0, /device:TPU:0, one launch (start us, length us, event | category | flops | bytes accessed | tf_op | source)
XLA Modules:
  0.0 981.0 jit_solution(7728629565180497052)
XLA Ops:
  18.8 5.3 copy.216
  24.1 5.3 copy.214
  30.4 131.4 %while.42 = (s32[]{:T(128)}, f32[1,32,1600]{2,1,0:T(8,128)S(1)}, f32[4,1,32,1600]{3,2,1,0:T(8,128)}, bf16[4,1,32,1600]{3,2,1,0:T(8,128)(2,1)}, s32[]{:T(128)}, /...) while((s32[]{:T(128)}, f32[1,32,1600]{2,1,0:T(8,128)S(1)}, ...), condition=%wide.region_6.7_spmd, body=%wide.region_0.6_spmd.sunk | while | flops 344828992 | bytes 25776712 | solution.py:167
  32.1 10.4 %conditional.7 = (f32[1,32,1600]{2,1,0:T(8,128)S(1)}) conditional(s32[]{:T(128)} %convert_element_type.778, f32[1,32,1600]{2,1,0:T(8,128)S(1)} %get-tuple-element.1149, (f32[1,32,1600]{2,1,0:T(8,128)S(1)}, bf16[1600,832]{1,0:T(8,128)(2,1)}, bf16[1600,832]{1,0:T(8,128)(2,1)S(1)}, bf16[1600,832]{1,0:T(8,128)(2,1)}, bf16[832,1600]{1,0:T(8,128)(2,1)}) %tuple.167), branch_computations={%region_1.1_spmd, %region_2.5_spmd} | conditional | flops 344624192 | bytes 23596836 | solution.py:161
  45.4 7.6 collective-permute-done
  54.7 10.4 %conditional.7 = (f32[1,32,1600]{2,1,0:T(8,128)S(1)}) conditional(s32[]{:T(128)} %convert_element_type.778, f32[1,32,1600]{2,1,0:T(8,128)S(1)} %get-tuple-element.1149, (f32[1,32,1600]{2,1,0:T(8,128)S(1)}, bf16[1600,832]{1,0:T(8,128)(2,1)}, bf16[1600,832]{1,0:T(8,128)(2,1)S(1)}, bf16[1600,832]{1,0:T(8,128)(2,1)}, bf16[832,1600]{1,0:T(8,128)(2,1)}) %tuple.167), branch_computations={%region_1.1_spmd, %region_2.5_spmd} | conditional | flops 344624192 | bytes 23596836 | solution.py:161
  76.0 10.4 %conditional.7 = (f32[1,32,1600]{2,1,0:T(8,128)S(1)}) conditional(s32[]{:T(128)} %convert_element_type.778, f32[1,32,1600]{2,1,0:T(8,128)S(1)} %get-tuple-element.1149, (f32[1,32,1600]{2,1,0:T(8,128)S(1)}, bf16[1600,832]{1,0:T(8,128)(2,1)}, bf16[1600,832]{1,0:T(8,128)(2,1)S(1)}, bf16[1600,832]{1,0:T(8,128)(2,1)}, bf16[832,1600]{1,0:T(8,128)(2,1)}) %tuple.167), branch_computations={%region_1.1_spmd, %region_2.5_spmd} | conditional | flops 344624192 | bytes 23596836 | solution.py:161
  96.4 10.4 %conditional.7 = (f32[1,32,1600]{2,1,0:T(8,128)S(1)}) conditional(s32[]{:T(128)} %convert_element_type.778, f32[1,32,1600]{2,1,0:T(8,128)S(1)} %get-tuple-element.1149, (f32[1,32,1600]{2,1,0:T(8,128)S(1)}, bf16[1600,832]{1,0:T(8,128)(2,1)}, bf16[1600,832]{1,0:T(8,128)(2,1)S(1)}, bf16[1600,832]{1,0:T(8,128)(2,1)}, bf16[832,1600]{1,0:T(8,128)(2,1)}) %tuple.167), branch_computations={%region_1.1_spmd, %region_2.5_spmd} | conditional | flops 344624192 | bytes 23596836 | solution.py:161
  116.2 14.8 %collective-permute-start = (f32[1,32,1600]{2,1,0:T(8,128)S(1)}, f32[1,32,1600]{2,1,0:T(8,128)S(1)}, u32[]{:S(2)}, u32[]{:S(2)}) collective-permute-start(f32[1,32,1600]{2,1,0:T(8,128)S(1)} %get-tuple-element.1302), channel_id=1, source_target_pairs={{0,4},{4,8},{8,12},{1,5},{5,9},{9,13},{2,6},{6,10},{10,14},{3,7},{... | collective-permute-start | bytes 614408 | tf_op jit(solution)/shard_map/while/body/eval_jaxpr/ppermute | solution.py:18
  145.5 12.9 %collective-permute-start = (f32[1,32,1600]{2,1,0:T(8,128)S(1)}, f32[1,32,1600]{2,1,0:T(8,128)S(1)}, u32[]{:S(2)}, u32[]{:S(2)}) collective-permute-start(f32[1,32,1600]{2,1,0:T(8,128)S(1)} %get-tuple-element.1302), channel_id=1, source_target_pairs={{0,4},{4,8},{8,12},{1,5},{5,9},{9,13},{2,6},{6,10},{10,14},{3,7},{... | collective-permute-start | bytes 614408 | tf_op jit(solution)/shard_map/while/body/eval_jaxpr/ppermute | solution.py:18
  170.1 31.5 %all_gather.11 = bf16[128,196]{1,0:T(8,128)(2,1)S(1)} all-gather(bf16[8,196]{1,0:T(8,128)(2,1)S(1)} %copy-done.20), channel_id=1, replica_groups=mesh['group'=2,'section'=4,'dp'=4] {'section','dp'}, dimensions={0}, use_global_device_ids=true | all-gather | bytes 53312 | tf_op jit(solution)/shard_map/all_gather | solution.py:141
  201.6 17.9 %all_gather.10 = bf16[4,128,128]{1,0,2:T(4,128)(2,1)S(1)} all-gather(bf16[4,128,8]{1,0,2:T(4,128)(2,1)S(1)} %copy.217), channel_id=1, replica_groups=mesh['group'=2,'section'=4,'dp'=4] {'section','dp'}, dimensions={2}, use_global_device_ids=true | all-gather | bytes 139264 | tf_op jit(solution)/shard_map/all_gather | solution.py:140
  219.5 4.9 conditional.3
  228.7 75.9 %all-reduce.11.cloned.1.call-done = bf16[4,128,128]{2,1,0:T(8,128)(2,1)} async-done(((bf16[4,128,128]{2,1,0:T(8,128)(2,1)}), bf16[4,128,128]{2,1,0:T(8,128)(2,1)}) %all-reduce.11.cloned.1.call-update) | async-done | bytes 131088 | tf_op jit(solution)/shard_map/psum | solution.py:23
  315.7 278.6 %while.43 = (s32[]{:T(128)}, f32[1,32,1600]{2,1,0:T(8,128)S(1)}, bf16[4,3,32,832]{3,2,0,1:T(8,128)(2,1)}, bf16[4,32,1600]{2,1,0:T(8,128)(2,1)}, bf16[4,32,832]{2...) while((s32[]{:T(128)}, f32[1,32,1600]{2,1,0:T(8,128)S(1)}, ...), condition=%wide.region_24.25_spmd.clone, body=%wide.region_16.24_spmd.clone.sunk | while | flops 608857152 | bytes 61259056 | solution.py:275
  344.9 87.1 %collective-permute-done.1 = bf16[1,32,1600]{2,1,0:T(8,128)(2,1)S(1)} collective-permute-done((bf16[1,32,1600]{2,1,0:T(8,128)(2,1)}, bf16[1,32,1600]{2,1,0:T(8,128)(2,1)S(1)}, u32[]{:S(2)}, u32[]{:S(2)}) %collective-permute-start.1) | collective-permute-done | bytes 102432 | tf_op jit(solution)/shard_map/while/body/eval_jaxpr/ppermute | solution.py:18
  433.8 31.3 %conditional.8 = (bf16[1,32,1600]{2,1,0:T(8,128)(2,1)}, bf16[1,3,32,832]{3,2,1,0:T(8,128)(2,1)S(1)}, bf16[1,32,1600]{2,1,0:T(8,128)(2,1)}, bf16[1,32,832]{2,1,0:T(8,128)(2,1)S(1)}) conditional(s32[]{:T(128)} %convert_element_type.779, () %tuple.170, (f32[1,32,1600]{2,1,0:T(8,128)S(1)}, bf16[832,1600]{1,0:T(8,128)(2,1)}, ...), branch_computations={%region_17.17_spmd, %region_18.23_spmd} | conditional | flops 608443456 | bytes 57541052 | solution.py:254
  474.6 31.3 %conditional.8 = (bf16[1,32,1600]{2,1,0:T(8,128)(2,1)}, bf16[1,3,32,832]{3,2,1,0:T(8,128)(2,1)S(1)}, bf16[1,32,1600]{2,1,0:T(8,128)(2,1)}, bf16[1,32,832]{2,1,0:T(8,128)(2,1)S(1)}) conditional(s32[]{:T(128)} %convert_element_type.779, () %tuple.170, (f32[1,32,1600]{2,1,0:T(8,128)S(1)}, bf16[832,1600]{1,0:T(8,128)(2,1)}, ...), branch_computations={%region_17.17_spmd, %region_18.23_spmd} | conditional | flops 608443456 | bytes 57541052 | solution.py:254
  515.3 31.3 %conditional.8 = (bf16[1,32,1600]{2,1,0:T(8,128)(2,1)}, bf16[1,3,32,832]{3,2,1,0:T(8,128)(2,1)S(1)}, bf16[1,32,1600]{2,1,0:T(8,128)(2,1)}, bf16[1,32,832]{2,1,0:T(8,128)(2,1)S(1)}) conditional(s32[]{:T(128)} %convert_element_type.779, () %tuple.170, (f32[1,32,1600]{2,1,0:T(8,128)S(1)}, bf16[832,1600]{1,0:T(8,128)(2,1)}, ...), branch_computations={%region_17.17_spmd, %region_18.23_spmd} | conditional | flops 608443456 | bytes 57541052 | solution.py:254
  556.0 31.3 %conditional.8 = (bf16[1,32,1600]{2,1,0:T(8,128)(2,1)}, bf16[1,3,32,832]{3,2,1,0:T(8,128)(2,1)S(1)}, bf16[1,32,1600]{2,1,0:T(8,128)(2,1)}, bf16[1,32,832]{2,1,0:T(8,128)(2,1)S(1)}) conditional(s32[]{:T(128)} %convert_element_type.779, () %tuple.170, (f32[1,32,1600]{2,1,0:T(8,128)S(1)}, bf16[832,1600]{1,0:T(8,128)(2,1)}, ...), branch_computations={%region_17.17_spmd, %region_18.23_spmd} | conditional | flops 608443456 | bytes 57541052 | solution.py:254
  596.3 12.4 %copy.242 = bf16[1,1600,832]{2,0,1:T(2,128)(2,1)} copy(bf16[1,1600,832]{1,2,0:T(8,128)(2,1)S(1)} %fusion.92) | data formatting | bytes 5324800
  608.8 4.7 copy.332
  617.2 14.5 %copy.244 = bf16[1,1600,832]{2,0,1:T(2,128)(2,1)} copy(bf16[1,1600,832]{1,2,0:T(8,128)(2,1)} %fusion.93) | data formatting | bytes 5324800
  631.7 4.6 copy.331
  639.1 14.4 %copy.240 = bf16[1,1600,832]{2,0,1:T(2,128)(2,1)} copy(bf16[1,1600,832]{1,2,0:T(8,128)(2,1)} %fusion.91) | data formatting | bytes 5324800
  664.7 4.8 copy.229
  679.4 8.6 reduce-scatter.26.cloned.1.call-done
  690.7 35.9 %reduce-scatter.22.cloned.1.call-done = bf16[400,832]{1,0:T(8,128)(2,1)} async-done(((bf16[1600,832]{1,0:T(8,128)(2,1)}), bf16[400,832]{1,0:T(8,128)(2,1)}) %reduce-scatter.22.cloned.1.call-update) | async-done | bytes 665616
  729.4 90.1 %reduce-scatter.18.cloned.1.call-done = f32[5,1600,8]{1,0,2:T(8,128)} async-done(((f32[5,1600,128]{1,0,2:T(8,128)}), f32[5,1600,8]{1,0,2:T(8,128)}) %reduce-scatter.18.cloned.1.call-update) | async-done | bytes 256016 | tf_op jit(solution)/shard_map/reduce_scatter | solution.py:304
  821.3 56.8 %reduce-scatter.28.cloned.1.call-done = f32[8,196]{1,0:T(8,128)} async-done(((f32[128,196]{1,0:T(8,128)}), f32[8,196]{1,0:T(8,128)}) %reduce-scatter.28.cloned.1.call-update) | async-done | bytes 6288
  878.1 58.5 %reduce-scatter.20.cloned.1.call-done = f32[4,128,8]{1,2,0:T(8,128)} async-done(((f32[4,128,128]{1,2,0:T(8,128)}), f32[4,128,8]{1,2,0:T(8,128)}) %reduce-scatter.20.cloned.1.call-update) | async-done | bytes 16400 | tf_op jit(solution)/shard_map/reduce_scatter | solution.py:307
  936.6 37.6 %reduce-scatter.16.cloned.1.call-done = bf16[1,208,1600]{2,1,0:T(8,128)(2,1)} async-done(((bf16[1,832,1600]{2,1,0:T(8,128)(2,1)}), bf16[1,208,1600]{2,1,0:T(8,128)(2,1)}) %reduce-scatter.16.cloned.1.call-update) | async-done | bytes 665616 | tf_op jit(solution)/shard_map/reduce_scatter | solution.py:299
  (456 shorter events, 362.8 us)
Async XLA Ops:
  7.2 154.6 %all-gather.2.cloned.1.call-start = ((), (), s32[]{:S(2)}) async-start(), calls=%async_computation.7 | async-start | bytes 2263040 | tf_op jit(solution)/shard_map/all_gather | solution.py:139
  7.9 211.6 %all-reduce.13.cloned.1.call-start = ((), (), s32[]{:S(2)}) async-start(), calls=%async_computation.16 | async-start | bytes 262144 | tf_op jit(solution)/shard_map/psum | solution.py:23
  42.5 10.5 %collective-permute-start = (f32[1,32,1600]{2,1,0:T(8,128)S(1)}, f32[1,32,1600]{2,1,0:T(8,128)S(1)}, u32[]{:S(2)}, u32[]{:S(2)}) collective-permute-start(f32[1,32,1600]{2,1,0:T(8,128)S(1)} %get-tuple-element.1302), channel_id=1, source_target_pairs={{0,4},{4,8},{8,12},{1,5},{5,9},{9,13},{2,6},{6,10},{10,14},{3,7},{... | collective-permute-start | bytes 614408 | tf_op jit(solution)/shard_map/while/body/eval_jaxpr/ppermute | solution.py:18
  65.1 9.2 collective-permute-start
  86.4 8.3 collective-permute-start
  106.8 7.7 collective-permute-start
  116.2 18.1 %collective-permute-start = (f32[1,32,1600]{2,1,0:T(8,128)S(1)}, f32[1,32,1600]{2,1,0:T(8,128)S(1)}, u32[]{:S(2)}, u32[]{:S(2)}) collective-permute-start(f32[1,32,1600]{2,1,0:T(8,128)S(1)} %get-tuple-element.1302), channel_id=1, source_target_pairs={{0,4},{4,8},{8,12},{1,5},{5,9},{9,13},{2,6},{6,10},{10,14},{3,7},{... | collective-permute-start | bytes 614408 | tf_op jit(solution)/shard_map/while/body/eval_jaxpr/ppermute | solution.py:18
  136.1 7.7 collective-permute-start
  145.5 16.2 %collective-permute-start = (f32[1,32,1600]{2,1,0:T(8,128)S(1)}, f32[1,32,1600]{2,1,0:T(8,128)S(1)}, u32[]{:S(2)}, u32[]{:S(2)}) collective-permute-start(f32[1,32,1600]{2,1,0:T(8,128)S(1)} %get-tuple-element.1302), channel_id=1, source_target_pairs={{0,4},{4,8},{8,12},{1,5},{5,9},{9,13},{2,6},{6,10},{10,14},{3,7},{... | collective-permute-start | bytes 614408 | tf_op jit(solution)/shard_map/while/body/eval_jaxpr/ppermute | solution.py:18
  161.7 8.3 copy-start.18
  161.7 8.3 copy-start.20
  161.7 57.7 %copy-start.16 = (s32[4,1,384]{2,1,0:T(1,128)S(1)}, s32[4,1,384]{2,1,0:T(1,128)}, u32[]{:S(2)}) copy-start(s32[4,1,384]{2,1,0:T(1,128)} %param.23) | copy-start | bytes 18436
  161.7 57.7 %copy-start.17 = (s32[4,1,384]{2,1,0:T(1,128)S(1)}, s32[4,1,384]{2,1,0:T(1,128)}, u32[]{:S(2)}) copy-start(s32[4,1,384]{2,1,0:T(1,128)} %param.24) | copy-start | bytes 18436
  161.8 57.7 %copy-start.19 = (f32[4,1,384]{2,1,0:T(1,128)S(1)}, f32[4,1,384]{2,1,0:T(1,128)}, u32[]{:S(2)}) copy-start(f32[4,1,384]{2,1,0:T(1,128)} %param.25) | copy-start | bytes 18436
  170.0 134.6 %all-reduce.11.cloned.1.call-start = ((), (), s32[]{:S(2)}) async-start(), calls=%async_computation.8 | async-start | bytes 262144 | tf_op jit(solution)/shard_map/psum | solution.py:23
  226.0 450.6 %reduce-scatter.24.cloned.1.call-start = ((), (), s32[]{:S(2)}) async-start(), calls=%async_computation.13 | async-start | bytes 3584000
  318.8 6.8 collective-permute-start.1
  328.8 6.8 collective-permute-start.1
  338.9 93.1 %collective-permute-start.1 = (bf16[1,32,1600]{2,1,0:T(8,128)(2,1)}, bf16[1,32,1600]{2,1,0:T(8,128)(2,1)S(1)}, u32[]{:S(2)}, u32[]{:S(2)}) collective-permute-start(bf16[1,32,1600]{2,1,0:T(8,128)(2,1)} %get-tuple-element.1167), channel_id=1, source_target_pairs={{4,0},{8,4},{12,8},{5,1},{9,5},{13,9},{6,2},{10,6},{14,10},{7,3},{... | collective-permute-start | bytes 307208 | tf_op jit(solution)/shard_map/while/body/eval_jaxpr/ppermute | solution.py:18
  461.2 3.8 copy-start.7
  465.1 7.6 collective-permute-start.1
  505.9 7.6 collective-permute-start.1
  542.7 3.8 copy-start.7
  546.6 7.6 collective-permute-start.1
  587.3 7.0 collective-permute-start.1
  613.5 74.4 %reduce-scatter.26.cloned.1.call-start = ((), (), s32[]{:S(2)}) async-start(), calls=%async_computation.14 | async-start | bytes 3584000
  636.4 90.3 %reduce-scatter.22.cloned.1.call-start = ((), (), s32[]{:S(2)}) async-start(), calls=%async_computation.12 | async-start | bytes 3584000
  658.1 6.5 copy-start.11
  658.2 161.4 %reduce-scatter.18.cloned.1.call-start = ((), (), s32[]{:S(2)}) async-start(), calls=%async_computation.10 | async-start | bytes 7241728 | tf_op jit(solution)/shard_map/reduce_scatter | solution.py:304
  669.5 208.6 %reduce-scatter.28.cloned.1.call-start = ((), (), s32[]{:S(2)}) async-start(), calls=%async_computation.15 | async-start | bytes 139264
  671.2 265.4 %reduce-scatter.20.cloned.1.call-start = ((), (), s32[]{:S(2)}) async-start(), calls=%async_computation.11 | async-start | bytes 278528 | tf_op jit(solution)/shard_map/reduce_scatter | solution.py:307
  673.0 301.2 %reduce-scatter.16.cloned.1.call-start = ((), (), s32[]{:S(2)}) async-start(), calls=%async_computation.9 | async-start | bytes 3461120 | tf_op jit(solution)/shard_map/reduce_scatter | solution.py:299
  (35 other events, 96.7 us)
Sparse Core Ops, SparseCore 0:
  10.2 44.1 all-gather.1
  170.1 45.8 all-reduce.12
  226.1 78.4 all-reduce.10
  613.6 35.4 reduce-scatter.23
  651.7 36.2 reduce-scatter.25
  690.3 36.2 reduce-scatter.21
  731.1 88.3 reduce-scatter.17
  823.6 54.5 reduce-scatter.27
  882.2 54.3 reduce-scatter.19
  939.6 34.5 reduce-scatter.15
where the time goes:
time: 987 us; the launch traced here: 981 us
  waiting for transfers between devices  475 us (48%)
  matrix products  149 us (15%)
  local copies, waits for them, and re-layouts  142 us (14%)
  other arithmetic  88.3 us (9%)
  starting transfers between devices  56.4 us (6%)
  blocking collectives  49.4 us (5%)
  between operations  19.4 us (2%)
    ppermute x14, waiting for transfers between devices, passed_along(): return lax.ppermute(block, axis, route)  111 us
    unnamed x14, waiting for transfers between devices  102 us
    reduce_scatter x1, waiting for transfers between devices, on_device(): lax.psum_scatter(grad_reassemble.astype(jnp.float32), ('section', 'dp'),...  90.1 us
    unnamed x43, local copies, waits for them, and re-layouts  85.7 us
    psum x2, waiting for transfers between devices, broadcast(): return lax.psum(kept, axis)  75.9 us
    select_n x42, other arithmetic, put_slot(): return jnp.where(active, updated, store_array)  65.6 us
    reduce_scatter x1, waiting for transfers between devices, on_device(): lax.psum_scatter(grad_merging.astype(jnp.float32), ('section', 'dp'), sca...  58.5 us
    ppermute x14, starting transfers between devices, passed_along(): return lax.ppermute(block, axis, route)  55.6 us
  transfers between devices with their start and end apart: 24, of which 20 were waited for; matrix products, arithmetic and copies ran while one was open for 20% of the time, Pallas kernels for 0%

commit v1 on v0

v1 whole, which is shorter than its diff:
```python
import functools
import math

import jax
import jax.numpy as jnp
from jax import lax
from jax.experimental import pallas as pl
from jax.experimental.pallas import tpu as pltpu
from jax.sharding import PartitionSpec as P

HEADS = 13
NHOOK = 4
EPS = 1e-06

F32 = jnp.float32
BF16 = jnp.bfloat16


def mm(a, b):
    return lax.dot_general(a, b, (((1,), (0,)), ((), ())), preferred_element_type=F32)


def mm_nt(a, b):
    return lax.dot_general(a, b, (((1,), (1,)), ((), ())), preferred_element_type=F32)


def mm_tn(a, b):
    return lax.dot_general(a, b, (((0,), (0,)), ((), ())), preferred_element_type=F32)


def exact_mm(a, b, dims):
    return lax.dot_general(
        a, b, (dims, ((), ())), preferred_element_type=F32, precision=lax.Precision.HIGHEST
    )


def sigmoid(v):
    return 1.0 / (1.0 + jnp.exp(-v))


def body(
    sections, dps,
    tok, pix, msk, dep, hook, wq, wk, wv, wo, rea, mer, pred,
    normed_g, mixed_g, dq_g, dk_g, dv_g, cot_g, feat_g, dr_g, hd_g,
    x_st, q_st, k_st, v_st, p_st, xr_in, xr_out, gr_in, gr_out, top_g, dd_st, x_cot,
    fsend, frecv, bsend, brecv, gsend, grecv,
):
    micro, rows, width = tok.shape
    inner = wq.shape[1]
    hw = inner // HEADS
    feats = rea.shape[1]
    pixels = pred.shape[1]
    points = pix.shape[2]
    pad = xr_in.shape[2] - NHOOK * feats
    big = HEADS * rows
    s = lax.axis_index("section")
    last = sections - 1

    d = lax.axis_index("dp")
    normed_o, mixed_o, dq_o, dk_o, dv_o, cot_o, feat_o, dr_o, hd_o = [
        ref.at[d]
        for ref in (normed_g, mixed_g, dq_g, dk_g, dv_g, cot_g, feat_g, dr_g, hd_g)
    ]
    barrier = pltpu.get_barrier_semaphore()
    for hop in range(1, dps):
        pl.semaphore_signal(barrier, inc=1, device_id={"dp": lax.rem(d + hop, dps)},
                            device_id_type=pl.DeviceIdType.MESH)

    @pl.when(s > 0)
    def _():
        pl.semaphore_signal(barrier, inc=1, device_id={"section": s - 1},
                            device_id_type=pl.DeviceIdType.MESH)

    @pl.when(s < last)
    def _():
        pl.semaphore_signal(barrier, inc=1, device_id={"section": s + 1},
                            device_id_type=pl.DeviceIdType.MESH)

    pl.semaphore_wait(barrier, dps - 1 + jnp.where(s > 0, 1, 0) + jnp.where(s < last, 1, 0))

    owned = [hook[j] == s for j in range(NHOOK)]

    def fwd_copy(m):
        return pltpu.make_async_remote_copy(
            src_ref=xr_out.at[m], dst_ref=xr_in.at[m],
            send_sem=fsend.at[m], recv_sem=frecv.at[m],
            device_id={"section": s + 1}, device_id_type=pl.DeviceIdType.MESH)

    def bwd_copy(m):
        return pltpu.make_async_remote_copy(
            src_ref=gr_out.at[m], dst_ref=gr_in.at[m],
            send_sem=bsend.at[m], recv_sem=brecv.at[m],
            device_id={"section": s - 1}, device_id_type=pl.DeviceIdType.MESH)

    def spread_copy(place, ref, m, hop):
        return pltpu.make_async_remote_copy(
            src_ref=ref.at[d, m], dst_ref=ref.at[d, m],
            send_sem=gsend.at[place, m, hop], recv_sem=grecv.at[place, m, hop],
            device_id={"dp": lax.rem(d + hop, dps)}, device_id_type=pl.DeviceIdType.MESH)

    early = ((0, normed_g), (1, mixed_g), (2, feat_g))
    late = ((3, cot_g), (4, dq_g), (5, dk_g), (6, dv_g), (7, dr_g))
    heads = ((8, hd_g),)

    def send_group(group, m):
        for place, ref in group:
            for hop in range(1, dps):
                spread_copy(place, ref, m, hop).start()

    def wait_group(group, m):
        for place, ref in group:
            for hop in range(1, dps):
                spread_copy(place, ref, m, hop).wait()

    def head_mask():
        row_head = lax.broadcasted_iota(jnp.int32, (HEADS, rows, inner), 0)
        col = lax.broadcasted_iota(jnp.int32, (HEADS, rows, inner), 2)
        lo = row_head * hw
        return ((col >= lo) & (col < lo + hw)).reshape(big, inner)

    def spread(a, mask):
        tiled = jnp.broadcast_to(a[None], (HEADS,) + a.shape).reshape(big, inner)
        return jnp.where(mask, tiled, 0.0).astype(BF16)

    def gathered(a, mask):
        return jnp.sum(jnp.where(mask, a, 0.0).reshape(HEADS, rows, inner), axis=0)

    def forward(m, carry):
        @pl.when(s > 0)
        def _():
            fwd_copy(m).wait_recv()

        first = s == 0
        arrived = xr_in[m]
        x = jnp.where(first, tok[m].astype(F32), arrived[:, :width].astype(F32))
        x_st[m] = x
        inv = lax.rsqrt(jnp.mean(x * x, axis=-1, keepdims=True) + EPS)
        normed = (x * inv).astype(BF16)
        normed_o[m] = normed
        q = mm(normed, wq[...])
        k = mm(normed, wk[...]).astype(BF16)
        v = mm(normed, wv[...]).astype(BF16)
        q_st[m] = q.astype(BF16)
        k_st[m] = k
        v_st[m] = v
        mask = head_mask()
        scores = mm_nt(spread(q, mask), k) * (1.0 / math.sqrt(hw))
        top = jnp.max(scores, axis=-1, keepdims=True)
        e = jnp.exp(scores - top)
        p = e / jnp.sum(e, axis=-1, keepdims=True)
        p_st[m] = p
        mixed = gathered(mm(p.astype(BF16), v), mask).astype(BF16)
        mixed_o[m] = mixed
        y = x + mm(mixed, wo[...])
        feat = y.astype(BF16)
        feat_o[m] = feat
        xr_out[m, :, :width] = feat
        for j in range(NHOOK):
            before = arrived[:, pad + j * feats:pad + (j + 1) * feats].astype(F32)
            mine = mm_nt(feat, rea[j])
            xr_out[m, :, pad + j * feats:pad + (j + 1) * feats] = jnp.where(
                owned[j], mine, before).astype(BF16)

        @pl.when(s < last)
        def _():
            fwd_copy(m).start()

        send_group(early, m)
        return carry

    lax.fori_loop(0, micro, forward, 0)

    @pl.when(s < last)
    def _():
        hd_g[...] = jnp.zeros_like(hd_g)
        dr_o[:, :, NHOOK * feats:] = jnp.zeros((micro, rows, feats), BF16)

    @pl.when(s == last)
    def _():
        total = micro * rows
        r_all = xr_in[:, :, pad:].reshape(total, NHOOK * feats)
        r = [r_all[:, j * feats:(j + 1) * feats].astype(F32) for j in range(NHOOK)]
        r_top = mm_nt(feat_o[...].reshape(total, width), rea[NHOOK]).astype(BF16).astype(F32)
        merged = [None] * NHOOK + [r_top]
        gate = [None] * (NHOOK + 1)
        act = [None] * (NHOOK + 1)
        for j in range(NHOOK, -1, -1):
            gate[j] = sigmoid(merged[j])
            act[j] = (merged[j] * gate[j]).astype(BF16)
            if j > 0:
                merged[j - 1] = r[j - 1] + mm_nt(act[j], mer[j - 1])
        depth = mm(act[0], pred[...])
        edge = lax.broadcasted_iota(jnp.int32, (rows, points), 0) * pixels
        place = lax.broadcasted_iota(jnp.int32, (pixels, points), 0)
        for m in range(micro):
            where = jnp.broadcast_to(pix[m], (rows, points))
            over = where >= edge
            token_hot = (over & (where < edge + pixels)).astype(F32)
            token_id = jnp.sum(over.astype(F32), axis=0, keepdims=True).astype(jnp.int32) - 1
            pix_hot = (place == (pix[m] - token_id * pixels)).astype(F32)
            spot = exact_mm(depth[m * rows:(m + 1) * rows], pix_hot, ((1,), (0,)))
            picked = jnp.sum(spot * token_hot, axis=0, keepdims=True)
            valid = msk[m].astype(F32)
            count = jnp.sum(valid, axis=1, keepdims=True)
            slope = 2.0 * (picked - dep[m]) * valid * valid / count
            dd_st[m * rows:(m + 1) * rows, :] = exact_mm(token_hot * slope, pix_hot, ((1,), (1,)))
        dd = dd_st[...].astype(BF16)
        hd_o[:, :, (2 * NHOOK + 1) * feats:] = dd.reshape(micro, rows, pixels)
        for j in range(NHOOK + 1):
            hd_o[:, :, (NHOOK + j) * feats:(NHOOK + j + 1) * feats] = act[j].reshape(
                micro, rows, feats)
        d_act = mm_nt(dd, pred[...]).astype(BF16).astype(F32)
        for j in range(NHOOK + 1):
            d_merged = d_act * (gate[j] * (1.0 + merged[j] * (1.0 - gate[j])))
            d_low = d_merged.astype(BF16)
            if j < NHOOK:
                gr_out[:, :, pad + j * feats:pad + (j + 1) * feats] = d_low.reshape(
                    micro, rows, feats)
                hd_o[:, :, j * feats:(j + 1) * feats] = d_low.reshape(micro, rows, feats)
                d_act = mm(d_low, mer[j]).astype(BF16).astype(F32)
                dr_o[:, :, j * feats:(j + 1) * feats] = jnp.zeros((micro, rows, feats), BF16)
            else:
                dr_o[:, :, j * feats:(j + 1) * feats] = d_low.reshape(micro, rows, feats)
                top_g[...] = mm(d_low, rea[NHOOK]).reshape(micro, rows, width).astype(BF16)

        for m in range(micro):
            send_group(heads, m)

    def backward(m, carry):
        @pl.when(s < last)
        def _():
            bwd_copy(m).wait_recv()
            arrived = gr_in[m]
            g = arrived[:, :width].astype(F32)
            for j in range(NHOOK):
                part = arrived[:, pad + j * feats:pad + (j + 1) * feats].astype(F32)
                gr_out[m, :, pad + j * feats:pad + (j + 1) * feats] = part.astype(BF16)
                kept = jnp.where(owned[j], part, 0.0).astype(BF16)
                dr_o[m, :, j * feats:(j + 1) * feats] = kept
                g = g + mm(kept, rea[j])
            x_cot[...] = g

        @pl.when(s == last)
        def _():
            x_cot[...] = top_g[m].astype(F32)

        g = x_cot[...]
        g_low = g.astype(BF16)
        cot_o[m] = g_low
        d_mixed = mm_nt(g_low, wo[...])
        mask = head_mask()
        q_big = spread(q_st[m].astype(F32), mask)
        dm_big = spread(d_mixed, mask)
        p = p_st[m]
        dp = mm_nt(dm_big, v_st[m]).astype(BF16).astype(F32)
        ds = (p * (dp - jnp.sum(dp * p, axis=-1, keepdims=True)) * (1.0 / math.sqrt(hw)))
        ds = ds.astype(BF16)
        dv = mm_tn(p.astype(BF16), dm_big).astype(BF16)
        dk = mm_tn(ds, q_big).astype(BF16)
        dq = gathered(mm(ds, k_st[m]), mask).astype(BF16)
        dq_o[m] = dq
        dk_o[m] = dk
        dv_o[m] = dv

        @pl.when(s > 0)
        def _():
            dn = mm_nt(dq, wq[...]) + mm_nt(dk, wk[...]) + mm_nt(dv, wv[...])
            x = x_st[m]
            inv = lax.rsqrt(jnp.mean(x * x, axis=-1, keepdims=True) + EPS)
            along = jnp.mean(dn * x, axis=-1, keepdims=True)
            dx = x_cot[...] + inv * dn - x * (inv * inv * inv * along)
            gr_out[m, :, :width] = dx.astype(BF16)
            bwd_copy(m).start()

        send_group(late, m)
        return carry

    lax.fori_loop(0, micro, backward, 0)

    @pl.when(s < last)
    def _():
        for m in range(micro):
            fwd_copy(m).wait_send()

    @pl.when(s == last)
    def _():
        for m in range(micro):
            wait_group(heads, m)

    @pl.when(s > 0)
    def _():
        for m in range(micro):
            bwd_copy(m).wait_send()

    def settle(m, carry):
        wait_group(early, m)
        wait_group(late, m)
        return carry

    lax.fori_loop(0, micro, settle, 0)


def pipeline(sections, dps, tok, pix, msk, dep, hook, wq, wk, wv, wo, rea, mer, pred):
    micro, rows, width = tok.shape
    inner = wq.shape[1]
    feats = rea.shape[1]
    pixels = pred.shape[1]
    pad = -(-width // 128) * 128
    wide = pad + NHOOK * feats
    vm = pl.BlockSpec(memory_space=pltpu.VMEM)
    sm = pl.BlockSpec(memory_space=pltpu.SMEM)

    def low(*shape):
        return jax.ShapeDtypeStruct((dps,) + shape, BF16)

    return pl.pallas_call(
        functools.partial(body, sections, dps),
        out_shape=(
            low(micro, rows, width), low(micro, rows, inner),
            low(micro, rows, inner), low(micro, rows, inner), low(micro, rows, inner),
            low(micro, rows, width), low(micro, rows, width),
            low(micro, rows, (NHOOK + 1) * feats),
            low(micro, rows, (2 * NHOOK + 1) * feats + pixels),
        ),
        in_specs=[vm, vm, vm, vm, sm] + [vm] * 7,
        out_specs=tuple([vm] * 9),
        scratch_shapes=[
            pltpu.VMEM((micro, rows, width), F32),
            pltpu.VMEM((micro, rows, inner), BF16),
            pltpu.VMEM((micro, rows, inner), BF16),
            pltpu.VMEM((micro, rows, inner), BF16),
            pltpu.VMEM((micro, HEADS * rows, rows), F32),
            pltpu.VMEM((micro, rows, wide), BF16),
            pltpu.VMEM((micro, rows, wide), BF16),
            pltpu.VMEM((micro, rows, wide), BF16),
            pltpu.VMEM((micro, rows, wide), BF16),
            pltpu.VMEM((micro, rows, width), BF16),
            pltpu.VMEM((micro * rows, pixels), F32),
            pltpu.VMEM((rows, width), F32),
            pltpu.SemaphoreType.DMA((micro,)),
            pltpu.SemaphoreType.DMA((micro,)),
            pltpu.SemaphoreType.DMA((micro,)),
            pltpu.SemaphoreType.DMA((micro,)),
            pltpu.SemaphoreType.DMA((9, micro, dps)),
            pltpu.SemaphoreType.DMA((9, micro, dps)),
        ],
        compiler_params=pltpu.CompilerParams(
            collective_id=0, has_side_effects=True, vmem_limit_bytes=56 * 1024 * 1024
        ),
    )(tok, pix, msk, dep, hook, wq, wk, wv, wo, rea, mer, pred)


def on_device(
    tokens, pixel_index, point_mask, point_depth, hook_section,
    w_query, w_key, w_value, w_output, reassemble, merging, predict,
):
    sections = lax.axis_size("section")
    dps = lax.axis_size("dp")
    d_index = lax.axis_index("dp")
    micro, images, tokens_in, width = tokens.shape
    rows = images * tokens_in
    points = pixel_index.shape[2]
    inner = w_query.shape[2]
    both = ("section", "dp")

    def whole(local):
        turned = jnp.swapaxes(local, 1, 2)
        every = lax.all_gather(turned, both, axis=0)
        return jnp.swapaxes(every, 0, 1).reshape(local.shape[0], -1, local.shape[1])

    rea = whole(reassemble)
    mer = whole(merging)
    pred = lax.all_gather(predict, both, axis=0, tiled=True)
    feats = rea.shape[1]

    normed, mixed, dq, dk, dv, cot, feat, dr, hd = pipeline(
        sections, dps,
        tokens.reshape(micro, rows, width),
        pixel_index.reshape(micro, 1, points),
        point_mask.reshape(micro, 1, points),
        point_depth.reshape(micro, 1, points),
        hook_section,
        w_query[0], w_key[0], w_value[0], w_output[0], rea, mer, pred,
    )
    total = micro * rows

    def dp_rows(a):
        return a.reshape(dps * total, a.shape[3])

    def own(a, size):
        return lax.dynamic_slice_in_dim(a, d_index * size, size, 1)

    normed_own = own(dp_rows(normed), width // dps)
    mixed_own = own(dp_rows(mixed), inner // dps)
    grad_query = mm_tn(normed_own, dp_rows(dq)).astype(BF16)
    grad_key = mm_tn(normed_own, dp_rows(dk)).astype(BF16)
    grad_value = mm_tn(normed_own, dp_rows(dv)).astype(BF16)
    grad_output = mm_tn(mixed_own, dp_rows(cot)).astype(BF16)

    piece = feats // (sections * dps)

    def columns(a, count):
        cut = a.reshape(dps * total, count, sections, dps, piece)
        return lax.dynamic_index_in_dim(cut, d_index, 3, keepdims=False)

    dr_own = columns(dp_rows(dr), NHOOK + 1).transpose(0, 2, 1, 3).reshape(dps * total, -1)
    part_rea = mm_tn(dr_own, dp_rows(feat)).reshape(sections, -1)
    hd_rows = dp_rows(hd)
    d_low = columns(hd_rows[:, :NHOOK * feats], NHOOK)
    acts = hd_rows[:, NHOOK * feats:(2 * NHOOK + 1) * feats].reshape(-1, NHOOK + 1, feats)
    part_mer = jnp.einsum("njsc,njf->sjcf", d_low, acts[:, 1:], preferred_element_type=F32)
    act_own = columns(acts[:, 0], 1).reshape(dps * total, sections * piece)
    part_pred = mm_tn(act_own, hd_rows[:, (2 * NHOOK + 1) * feats:])
    sent = jnp.concatenate(
        [part_rea, part_mer.reshape(sections, -1), part_pred.reshape(sections, -1)], axis=1)
    sent = jnp.pad(sent, ((0, 0), (0, -sent.shape[1] % 1024))).reshape(sections, -1, 128)
    mine = lax.psum_scatter(sent, "section", scatter_dimension=0, tiled=False).reshape(-1)
    cut_rea = (NHOOK + 1) * piece * width
    cut_mer = cut_rea + NHOOK * piece * feats
    grad_reassemble = mine[:cut_rea].reshape(NHOOK + 1, piece, width).swapaxes(1, 2)
    grad_merging = mine[cut_rea:cut_mer].reshape(NHOOK, piece, feats).swapaxes(1, 2)
    grad_predict = mine[cut_mer:cut_mer + piece * pred.shape[1]].reshape(piece, -1)
    return (
        grad_query[None], grad_key[None], grad_value[None], grad_output[None],
        grad_reassemble, grad_merging, grad_predict,
    )


def solution(mesh):
    placed = (
        P(None, ("group", "dp"), None, None),
        P(None, ("group", "dp"), None),
        P(None, ("group", "dp"), None),
        P(None, ("group", "dp"), None),
        P(),
        P("section", None, None),
        P("section", None, None),
        P("section", None, None),
        P("section", None, None),
        P(None, None, ("section", "dp")),
        P(None, None, ("section", "dp")),
        P(("section", "dp"), None),
    )
    return jax.shard_map(
        on_device,
        mesh=mesh,
        in_specs=placed,
        out_specs=(
            P(("group", "section"), "dp", None),
            P(("group", "section"), "dp", None),
            P(("group", "section"), "dp", None),
            P(("group", "section"), "dp", None),
            P("group", None, ("section", "dp")),
            P("group", None, ("section", "dp")),
            P(("group", "section", "dp"), None),
        ),
        check_vma=False,
    )
```

time: 987 us -> 306 us (0.31)
  waiting for transfers between devices: 475 us -> 67.7 us
  matrix products: 149 us -> 10.6 us
  Pallas kernels: 0 us -> 136 us
  local copies, waits for them, and re-layouts: 142 us -> 34.8 us
  other arithmetic: 88.3 us -> 0.25 us
  starting transfers between devices: 56.4 us -> 0.08 us
    reduce_scatter x3 -> x0, waiting for transfers between devices: 186 us -> none  [the longest x1 90.1 us: on_device(): lax.psum_scatter(grad_reassemble.astype(jnp.float32), ('section', 'dp'),...]
    pallas_call x0 -> x1, Pallas kernels: none -> 136 us  [pipeline(): pl.pallas_call(functools.partial(body, sections, dps), out_shape=(low(mic...]
    dot_general x84 -> x6, matrix products: 134 us -> 10.4 us  [mm_tn(): lax.dot_general(a, b, (((0,), (0,)), ((), ())), preferred_element_type=F32)]
    ppermute x14 -> x0, waiting for transfers between devices: 111 us -> none  [passed_along(): return lax.ppermute(block, axis, route)]
    psum x2 -> x0, waiting for transfers between devices: 75.9 us -> none  [broadcast(): return lax.psum(kept, axis)]
    unnamed x43 -> x28, local copies, waits for them, and re-layouts: 85.7 us -> 16.8 us
    select_n x43 -> x0, other arithmetic: 67.2 us -> none  [the longest x42 65.6 us: put_slot(): return jnp.where(active, updated, store_array)]
    ppermute x14 -> x0, starting transfers between devices: 55.6 us -> none  [passed_along(): return lax.ppermute(block, axis, route)]
  transfers between devices with their start and end apart: 24 -> 2, of which waited for: 20 -> 1; matrix products, arithmetic and copies ran while one was open for 20% -> 7% of each run, Pallas kernels for 0% -> 0%
where the time goes in v1:
time: 306 us
  Pallas kernels  136 us (44%)
  waiting for transfers between devices  67.7 us (22%)
  blocking collectives  42.5 us (14%)
  local copies, waits for them, and re-layouts  34.8 us (11%)
  between operations  14.2 us (5%)
  matrix products  10.6 us (3%)
    pallas_call x1, Pallas kernels, pipeline(): pl.pallas_call(functools.partial(body, sections, dps), out_shape=(low(mic...  136 us
    unnamed x3, waiting for transfers between devices  67.7 us
    all_gather x1, blocking collectives, whole(): every = lax.all_gather(turned, both, axis=0)  23.6 us
    all_gather x1, blocking collectives, on_device(): pred = lax.all_gather(predict, both, axis=0, tiled=True)  19 us
    unnamed x28, local copies, waits for them, and re-layouts  16.8 us
    dot_general x6, matrix products, mm_tn(): lax.dot_general(a, b, (((0,), (0,)), ((), ())), preferred_element_type=F32)  10.4 us
  transfers between devices with their start and end apart: 2, of which 1 were waited for; matrix products, arithmetic and copies ran while one was open for 7% of the time, Pallas kernels for 0%

profile of v1, /device:TPU:0, one launch (start us, length us, event | category | flops | bytes accessed | tf_op | source)
XLA Modules:
  0.0 305.7 jit_solution(5098044151223172425)
XLA Ops:
  7.2 0.7 all-gather.4.cloned.1.call-update
  8.0 5.4 %copy.36 = bf16[1,1600,832]{2,1,0:T(8,128)(2,1)} copy(bf16[1,1600,832]{1,2,0:T(8,128)(2,1)} %param.17) | data formatting | bytes 5324800 | tf_op args[5]
  13.4 3.5 %copy.37 = bf16[1,1600,832]{2,1,0:T(8,128)(2,1)} copy(bf16[1,1600,832]{1,2,0:T(8,128)(2,1)S(1)} %copy-done) | data formatting | bytes 5324800 | tf_op args[6]
  16.9 5.3 %copy.38 = bf16[1,1600,832]{2,1,0:T(8,128)(2,1)} copy(bf16[1,1600,832]{1,2,0:T(8,128)(2,1)} %param.19) | data formatting | bytes 5324800 | tf_op args[7]
  22.1 23.6 %all-gather.1 = bf16[64,8,128]{2,1,0:T(8,128)(2,1)S(1)} all-gather(bf16[4,8,128]{2,1,0:T(8,128)(2,1)S(1)} %bitcast.116), channel_id=3, replica_groups=mesh['group'=2,'section'=4,'dp'=4] {'section','dp'}, dimensions={0}, use_global_device_ids=true | all-gather | bytes 139264 | tf_op jit(solution)/shard_map/all_gather | solution.py:368
  45.7 0.7 copy.59
  46.4 19.0 %all_gather.19.pred = bf16[128,196]{1,0:T(8,128)(2,1)} all-gather(bf16[8,196]{1,0:T(8,128)(2,1)S(1)} %copy-done.8), channel_id=1, replica_groups=mesh['group'=2,'section'=4,'dp'=4] {'section','dp'}, dimensions={0}, use_global_device_ids=true | all-gather | bytes 53312 | tf_op jit(solution)/shard_map/all_gather | solution.py:373
  65.4 3.2 %copy.57 = bf16[16,5,8,1600]{3,2,0,1:T(8,128)(2,1)} copy(bf16[16,5,8,1600]{3,2,1,0:T(8,128)(2,1)} %bitcast.93) | data formatting | bytes 4096000 | tf_op jit(solution)/shard_map/all_gather | solution.py:368
  68.5 135.5 %shard_map.171 = (bf16[4,4,32,1600]{3,2,1,0:T(8,128)(2,1)}, bf16[4,4,32,832]{3,2,1,0:T(8,128)(2,1)}, bf16[4,4,32,832]{3,2,1,0:T(8,128)(2,1)}, bf16[4,4,32,832]{3...) custom-call(bf16[4,32,1600]{2,1,0:T(8,128)(2,1)} %bitcast.109, ...), custom_call_target="tpu_custom_call" | custom-call | tf_op jit(solution)/shard_map/pallas_call | solution.py:316
  204.0 1.1 slice.35
  205.2 1.1 slice.34
  206.3 0.3 copy.48
  206.6 1.2 fusion.9
  208.0 0.3 convolution_bitcast_fusion
  208.4 2.1 copy.41
  210.5 2.6 reshape_reshape.3
  213.1 1.9 fusion.22
  215.1 0.6 reshape.96
  215.7 0.2 fusion.4
  216.0 1.1 copy.58
  217.1 0.6 dynamic-slice
  217.8 0.2 copy-done.5
  218.1 1.6 fusion.1
  219.7 1.6 fusion.2
  221.2 1.6 fusion.3
  222.9 2.5 fusion
  225.4 67.0 %all-reduce.4.cloned.1.call-done = f32[4,552,128]{2,1,0:T(8,128)} async-done(((f32[4,552,128]{2,1,0:T(8,128)}), f32[4,552,128]{2,1,0:T(8,128)}) %all-reduce.4.cloned.1.call-update) | async-done | bytes 1130512
  292.4 1.5 constant_dynamic-slice_fusion
  293.9 0.8 reshape.104
  294.7 1.5 dynamic-slice_bitcast_fusion
  296.3 0.7 reshape.106
  297.0 1.9 dynamic-slice_bitcast_fusion.2
  (31 shorter events, 0.7 us)
Async XLA Ops:
  7.2 58.2 %all-gather.4.cloned.1.call-start = ((), (), s32[]{:S(2)}) async-start(), calls=%async_computation | async-start | bytes 2263040 | tf_op jit(solution)/shard_map/all_gather | solution.py:368
  7.9 284.5 %all-reduce.4.cloned.1.call-start = ((), (), s32[]{:S(2)}) async-start(), calls=%async_computation.1 | async-start | bytes 2260992
  8.0 5.4 %copy-start = (bf16[1,1600,832]{1,2,0:T(8,128)(2,1)S(1)}, bf16[1,1600,832]{1,2,0:T(8,128)(2,1)}, u32[]{:S(2)}) copy-start(bf16[1,1600,832]{1,2,0:T(8,128)(2,1)} %param.18) | copy-start | bytes 7987204
  16.9 5.3 %copy-start.7 = (bf16[4,128,8]{1,2,0:T(8,128)(2,1)S(1)}, bf16[4,128,8]{1,2,0:T(8,128)(2,1)}, u32[]{:S(2)}) copy-start(bf16[4,128,8]{1,2,0:T(8,128)(2,1)} %param.22) | copy-start | bytes 24580
  16.9 29.5 %copy-start.8 = (bf16[8,196]{1,0:T(8,128)(2,1)S(1)}, bf16[8,196]{1,0:T(8,128)(2,1)}, u32[]{:S(2)}) copy-start(bf16[8,196]{1,0:T(8,128)(2,1)} %param.23) | copy-start | bytes 9412
  206.5 1.9 copy-start.6
  215.9 1.2 copy-start.9
  215.9 1.9 copy-start.2
  216.0 2.1 copy-start.5
  217.1 2.6 copy-start.4
  219.6 1.6 copy-start.3
  221.2 1.6 copy-start.1
Sparse Core Ops, SparseCore 0:
  10.2 44.2 all-gather.3
  217.2 75.1 all-reduce.3

commit v2 on v1

--- a/solution.py
+++ b/solution.py
@@ -92,11 +92,15 @@
             send_sem=bsend.at[m], recv_sem=brecv.at[m],
             device_id={"section": s - 1}, device_id_type=pl.DeviceIdType.MESH)
 
+    mate = d + 1 - 2 * lax.rem(d, 2)
+
     def spread_copy(place, ref, m, hop):
+        block = d if hop % 2 == 0 or hop == 1 else lax.rem(d + dps - hop + 1, dps)
+        target = mate if hop % 2 == 1 else lax.rem(d + hop, dps)
         return pltpu.make_async_remote_copy(
-            src_ref=ref.at[d, m], dst_ref=ref.at[d, m],
+            src_ref=ref.at[block, m], dst_ref=ref.at[block, m],
             send_sem=gsend.at[place, m, hop], recv_sem=grecv.at[place, m, hop],
-            device_id={"dp": lax.rem(d + hop, dps)}, device_id_type=pl.DeviceIdType.MESH)
+            device_id={"dp": target}, device_id_type=pl.DeviceIdType.MESH)
 
     early = ((0, normed_g), (1, mixed_g), (2, feat_g))
     late = ((3, cot_g), (4, dq_g), (5, dk_g), (6, dv_g), (7, dr_g))
@@ -104,13 +108,22 @@
 
     def send_group(group, m):
         for place, ref in group:
-            for hop in range(1, dps):
+            for hop in [*range(2, dps, 2), 1]:
                 spread_copy(place, ref, m, hop).start()
+
+    def relay_group(group, m):
+        for place, ref in group:
+            for hop in range(2, dps, 2):
+                spread_copy(place, ref, m, hop).wait_recv()
+                spread_copy(place, ref, m, hop + 1).start()
 
     def wait_group(group, m):
         for place, ref in group:
             for hop in range(1, dps):
-                spread_copy(place, ref, m, hop).wait()
+                if hop % 2 == 0:
+                    spread_copy(place, ref, m, hop).wait_send()
+                else:
+                    spread_copy(place, ref, m, hop).wait()
 
     def head_mask():
         row_head = lax.broadcasted_iota(jnp.int32, (HEADS, rows, inner), 0)
@@ -273,9 +286,21 @@
             bwd_copy(m).start()
 
         send_group(late, m)
+        relay_group(early, m)
+
+        @pl.when(m > 0)
+        def _():
+            relay_group(late, m - 1)
+
         return carry
 
     lax.fori_loop(0, micro, backward, 0)
+    relay_group(late, micro - 1)
+
+    @pl.when(s == last)
+    def _():
+        for m in range(micro):
+            relay_group(heads, m)
 
     @pl.when(s < last)
     def _():

time: 306 us -> 272 us (0.89)
  waiting for transfers between devices: 67.7 us -> 44.7 us
  Pallas kernels: 136 us -> 124 us
    unnamed x3, waiting for transfers between devices: 67.7 us -> 44.7 us
    pallas_call x1, Pallas kernels: 136 us -> 124 us  [pipeline(): pl.pallas_call(functools.partial(body, sections, dps), out_shape=(low(mic...]
  transfers between devices with their start and end apart: 2 -> 2, of which waited for: 1 -> 1; matrix products, arithmetic and copies ran while one was open for 7% -> 8% of each run, Pallas kernels for 0% -> 0%
where the time goes in v2:
time: 272 us; the launch traced here: 271 us
  Pallas kernels  124 us (46%)
  waiting for transfers between devices  44.7 us (16%)
  blocking collectives  42.5 us (16%)
  local copies, waits for them, and re-layouts  34.8 us (13%)
  between operations  14.2 us (5%)
  matrix products  10.7 us (4%)
    pallas_call x1, Pallas kernels, pipeline(): pl.pallas_call(functools.partial(body, sections, dps), out_shape=(low(mic...  124 us
    unnamed x3, waiting for transfers between devices  44.7 us
    all_gather x1, blocking collectives, whole(): every = lax.all_gather(turned, both, axis=0)  23.6 us
    all_gather x1, blocking collectives, on_device(): pred = lax.all_gather(predict, both, axis=0, tiled=True)  19 us
    unnamed x28, local copies, waits for them, and re-layouts  16.8 us
    dot_general x6, matrix products, mm_tn(): lax.dot_general(a, b, (((0,), (0,)), ((), ())), preferred_element_type=F32)  10.4 us
  transfers between devices with their start and end apart: 2, of which 1 were waited for; matrix products, arithmetic and copies ran while one was open for 8% of the time, Pallas kernels for 0%

profile of v2, /device:TPU:0, one launch (start us, length us, event | category | flops | bytes accessed | tf_op | source)
XLA Modules:
  0.0 271.0 jit_solution(5208805381674755115)
XLA Ops:
  7.2 0.7 all-gather.4.cloned.1.call-update
  8.0 5.4 %copy.36 = bf16[1,1600,832]{2,1,0:T(8,128)(2,1)} copy(bf16[1,1600,832]{1,2,0:T(8,128)(2,1)} %param.17) | data formatting | bytes 5324800 | tf_op args[5]
  13.4 3.5 %copy.37 = bf16[1,1600,832]{2,1,0:T(8,128)(2,1)} copy(bf16[1,1600,832]{1,2,0:T(8,128)(2,1)S(1)} %copy-done) | data formatting | bytes 5324800 | tf_op args[6]
  16.9 5.3 %copy.38 = bf16[1,1600,832]{2,1,0:T(8,128)(2,1)} copy(bf16[1,1600,832]{1,2,0:T(8,128)(2,1)} %param.19) | data formatting | bytes 5324800 | tf_op args[7]
  22.1 23.6 %all-gather.1 = bf16[64,8,128]{2,1,0:T(8,128)(2,1)S(1)} all-gather(bf16[4,8,128]{2,1,0:T(8,128)(2,1)S(1)} %bitcast.116), channel_id=3, replica_groups=mesh['group'=2,'section'=4,'dp'=4] {'section','dp'}, dimensions={0}, use_global_device_ids=true | all-gather | bytes 139264 | tf_op jit(solution)/shard_map/all_gather | solution.py:393
  45.7 0.7 copy.59
  46.4 19.0 %all_gather.19.pred = bf16[128,196]{1,0:T(8,128)(2,1)} all-gather(bf16[8,196]{1,0:T(8,128)(2,1)S(1)} %copy-done.8), channel_id=1, replica_groups=mesh['group'=2,'section'=4,'dp'=4] {'section','dp'}, dimensions={0}, use_global_device_ids=true | all-gather | bytes 53312 | tf_op jit(solution)/shard_map/all_gather | solution.py:398
  65.4 3.2 %copy.57 = bf16[16,5,8,1600]{3,2,0,1:T(8,128)(2,1)} copy(bf16[16,5,8,1600]{3,2,1,0:T(8,128)(2,1)} %bitcast.93) | data formatting | bytes 4096000 | tf_op jit(solution)/shard_map/all_gather | solution.py:393
  68.5 123.8 %shard_map.171 = (bf16[4,4,32,1600]{3,2,1,0:T(8,128)(2,1)}, bf16[4,4,32,832]{3,2,1,0:T(8,128)(2,1)}, bf16[4,4,32,832]{3,2,1,0:T(8,128)(2,1)}, bf16[4,4,32,832]{3...) custom-call(bf16[4,32,1600]{2,1,0:T(8,128)(2,1)} %bitcast.109, ...), custom_call_target="tpu_custom_call" | custom-call | tf_op jit(solution)/shard_map/pallas_call | solution.py:341
  192.4 1.1 slice.35
  193.5 1.1 slice.34
  194.6 0.3 copy.48
  194.9 1.2 fusion.9
  196.4 0.3 convolution_bitcast_fusion
  196.7 2.1 copy.41
  198.8 2.6 reshape_reshape.3
  201.5 1.9 fusion.22
  203.4 0.6 reshape.96
  204.0 0.2 fusion.4
  204.3 1.1 copy.58
  205.4 0.6 dynamic-slice
  206.2 0.2 copy-done.5
  206.4 1.6 fusion.1
  208.0 1.6 fusion.2
  209.6 1.6 fusion.3
  211.2 2.5 fusion
  213.7 44.0 %all-reduce.4.cloned.1.call-done = f32[4,552,128]{2,1,0:T(8,128)} async-done(((f32[4,552,128]{2,1,0:T(8,128)}), f32[4,552,128]{2,1,0:T(8,128)}) %all-reduce.4.cloned.1.call-update) | async-done | bytes 1130512
  257.7 1.5 constant_dynamic-slice_fusion
  259.2 0.8 reshape.104
  260.0 1.5 dynamic-slice_bitcast_fusion
  261.6 0.7 reshape.106
  262.3 1.9 dynamic-slice_bitcast_fusion.2
  (31 shorter events, 0.7 us)
Async XLA Ops:
  7.2 58.2 %all-gather.4.cloned.1.call-start = ((), (), s32[]{:S(2)}) async-start(), calls=%async_computation | async-start | bytes 2263040 | tf_op jit(solution)/shard_map/all_gather | solution.py:393
  7.9 249.8 %all-reduce.4.cloned.1.call-start = ((), (), s32[]{:S(2)}) async-start(), calls=%async_computation.1 | async-start | bytes 2260992
  8.0 5.4 %copy-start = (bf16[1,1600,832]{1,2,0:T(8,128)(2,1)S(1)}, bf16[1,1600,832]{1,2,0:T(8,128)(2,1)}, u32[]{:S(2)}) copy-start(bf16[1,1600,832]{1,2,0:T(8,128)(2,1)} %param.18) | copy-start | bytes 7987204
  16.9 5.3 %copy-start.7 = (bf16[4,128,8]{1,2,0:T(8,128)(2,1)S(1)}, bf16[4,128,8]{1,2,0:T(8,128)(2,1)}, u32[]{:S(2)}) copy-start(bf16[4,128,8]{1,2,0:T(8,128)(2,1)} %param.22) | copy-start | bytes 24580
  16.9 29.5 %copy-start.8 = (bf16[8,196]{1,0:T(8,128)(2,1)S(1)}, bf16[8,196]{1,0:T(8,128)(2,1)}, u32[]{:S(2)}) copy-start(bf16[8,196]{1,0:T(8,128)(2,1)} %param.23) | copy-start | bytes 9412
  194.9 1.9 copy-start.6
  204.3 1.2 copy-start.9
  204.3 1.9 copy-start.2
  204.3 2.1 copy-start.5
  205.4 2.6 copy-start.4
  208.0 1.6 copy-start.3
  209.6 1.6 copy-start.1
Sparse Core Ops, SparseCore 0:
  10.2 44.2 all-gather.3
  205.5 52.0 all-reduce.3
